TPU v7x, 32 devices: a whole 2x2x4 slice. The times are simulated.
32 devices in a mesh: gx: 16 (over z, y, core), gy: 2 (over x).
Axes of the slice: x: 2, y: 2, z: 4, core: 2. Of those that a mesh axis runs over, the one named last changes fastest.
Arguments:
- kernel: bfloat16 [32768, 512], P(('gx', 'gy')), may hold values from -0.25 to 0.25
- margin: bfloat16 [32768, 512], P(('gx', 'gy')), may hold values from -0.25 to 0.25
- hamiltonian: bfloat16 [32768, 512], P(('gx', 'gy')), may hold values from -9 to 9
- columns: int32 [512, 8], replicated, may hold values from -1 to 511, as said below
Outputs:
- gradient_term: float32 [32768, 512], P(('gx', 'gy'))
Inputs may be any that keep to these rules, and one draw needn't show every extreme that they name: `columns`: clusters are numbered device by device, 16 each, device number = gx index * (devices along gy) + gy index. Slot 0 of row i names i itself; the live ids of a row are distinct, live slots come first and the rest hold -1; every device has a row with all 8 slots live. A row of the device at (x, y) names only clusters of its own device and clusters number r + 4 * (2 p + q) (r < 4, counted within the device) of the device at (x + s, y + t), indices wrapping around, with s and t in -1, 0, 1, where p = 1 if s = -1, p = 0 if s = 1, either if s = 0, and likewise q from t.
All inputs are finite; a program needn't handle non-finite values.
Results may differ from a plain program's by a relative error of at most 0.005.
Values may be sent and summed in bfloat16 or wider, within the bound.
A program may use at most 128 MiB of HBM per device.

v0:
```python
import math

import jax
import jax.numpy as jnp
from jax import lax
from jax.sharding import PartitionSpec as P

BS = 64
NB = 8
EDGE = 4
BLK_DEV = 16


def extended_2(cells, sides, width):
    for axis, dim in sides:
        count = lax.axis_size(axis)
        head = lax.slice_in_dim(cells, 0, width, axis=dim)
        tail = lax.slice_in_dim(cells, cells.shape[dim] - width, cells.shape[dim], axis=dim)
        cells = jnp.concatenate(
            [
                lax.ppermute(tail, axis, [(i, (i + 1) % count) for i in range(count)]),
                cells,
                lax.ppermute(head, axis, [((i + 1) % count, i) for i in range(count)]),
            ],
            axis=dim,
        )
    return cells


def outgoing(matrix):
    return matrix.reshape(2, 2, EDGE * BS, NB * BS)


def row_layout(local, received):
    far_rows = received.reshape(-1, NB * BS)
    joined = jnp.concatenate([local, far_rows], axis=0)
    return joined.reshape(-1, BS, NB * BS)


def pattern_product(left, extended, position, mapping):
    row_count = left.shape[0] // BS
    group = math.gcd(row_count, 4)
    lefts = left.reshape(row_count // group, group, BS, NB, BS)
    places = position.reshape(row_count // group, group, NB)
    maps = mapping.reshape(row_count // group, group, NB, NB, NB)

    def product_rows(pieces):
        left_rows, place_rows, map_rows = pieces
        far_rows = extended[place_rows].reshape(group, NB, BS, NB, BS)
        moved = jnp.einsum(
            "iasct,iacb->iasbt", far_rows, map_rows, preferred_element_type=jnp.float32
        ).astype(jnp.bfloat16)
        return jnp.einsum("iras,iasbt->irbt", left_rows, moved, preferred_element_type=jnp.float32)

    result = lax.map(product_rows, (lefts, places, maps))
    return result.reshape(left.shape[0], NB * BS)


def body(kernel, margin, hamiltonian, columns):
    block_count = BLK_DEV
    gx_index = lax.axis_index("gx")
    gy_index = lax.axis_index("gy")
    along_gy = lax.axis_size("gy")
    first_block = (gx_index * along_gy + gy_index) * block_count
    own_columns = lax.dynamic_slice_in_dim(columns, first_block, block_count, 0)
    offsets = jnp.array([-1, 0, 0, 1], jnp.int32)
    corner_side = jnp.array([1, 0, 1, 0], jnp.int32)
    source_x = (gx_index + offsets) % lax.axis_size("gx")
    source_y = (gy_index + offsets) % along_gy
    owners = source_x[:, None] * along_gy + source_y[None, :]
    quadrant = (2 * corner_side[:, None] + corner_side[None, :]) * EDGE
    ghost_ids = (
        owners[:, :, None] * block_count
        + quadrant[:, :, None]
        + jnp.arange(EDGE, dtype=jnp.int32)[None, None, :]
    ).reshape(-1)
    extended_ids = jnp.concatenate(
        [first_block + jnp.arange(block_count, dtype=jnp.int32), ghost_ids]
    )
    extended_count = extended_ids.shape[0]
    extended_columns = columns[extended_ids]
    is_live = own_columns >= 0
    found = extended_ids[None, None, :] == own_columns[:, :, None]
    position = jnp.min(
        jnp.where(
            found, jnp.arange(extended_count, dtype=jnp.int32)[None, None, :], extended_count
        ),
        axis=2,
    )
    position = jnp.where(is_live, position, 0)
    far_columns = extended_columns[position]
    matched = (
        (far_columns[:, :, :, None] == own_columns[:, None, None, :])
        & is_live[:, :, None, None]
        & is_live[:, None, None, :]
    )
    mapping = matched.astype(jnp.bfloat16)
    margin_arrived = extended_2(outgoing(margin), (("gx", 0), ("gy", 1)), 1)
    margin_ext = row_layout(margin, margin_arrived)
    lead_product = pattern_product(kernel, margin_ext, position, mapping).astype(jnp.bfloat16)
    kernel_arrived = extended_2(outgoing(kernel), (("gx", 0), ("gy", 1)), 1)
    kernel_ext = row_layout(kernel, kernel_arrived)
    cubic = pattern_product(lead_product, kernel_ext, position, mapping).astype(jnp.bfloat16)
    cubic_arrived = extended_2(outgoing(cubic), (("gx", 0), ("gy", 1)), 1)
    fifth = pattern_product(lead_product, row_layout(cubic, cubic_arrived), position, mapping)
    purified = (3.0 * cubic.astype(jnp.float32) - 2.0 * fifth).astype(jnp.bfloat16)
    purified_arrived = extended_2(outgoing(purified), (("gx", 0), ("gy", 1)), 1)
    return pattern_product(hamiltonian, row_layout(purified, purified_arrived), position, mapping)


def solution(mesh):
    in_specs = (P(("gx", "gy"), None), P(("gx", "gy"), None), P(("gx", "gy"), None), P())
    out_specs = P(("gx", "gy"), None)
    return jax.shard_map(body, mesh=mesh, in_specs=in_specs, out_specs=out_specs, check_vma=False)
```

profile of v0, /device:TPU:1, one launch (start us, length us, event | category | flops | bytes accessed | tf_op | source)
XLA Modules:
  0.0 465.7 jit_solution(12248661435238604484)
XLA Ops:
  11.2 11.4 %collective-permute-done = bf16[1,2,256,512]{3,2,1,0:T(8,128)(2,1)S(1)} collective-permute-done((bf16[1,2,256,512]{3,2,1,0:T(8,128)(2,1)}, bf16[1,2,256,512]{3,2,1,0:T(8,128)(2,1)S(1)}, u32[]{:S(2)}, u32[]{:S(2)}) %collective-permute-start) | collective-permute-done | bytes 524320 | tf_op jit(solution)/shard_map/ppermute | solution.py:21
  42.1 12.7 %collective-permute-done.2 = bf16[4,1,256,512]{3,2,1,0:T(8,128)(2,1)} collective-permute-done((bf16[4,1,256,512]{3,2,1,0:T(8,128)(2,1)}, bf16[4,1,256,512]{3,2,1,0:T(8,128)(2,1)}, u32[]{:S(2)}, u32[]{:S(2)}) %collective-permute-start.2) | collective-permute-done | bytes 1048608 | tf_op jit(solution)/shard_map/ppermute | solution.py:21
  54.8 22.5 %collective-permute-done.3 = bf16[4,1,256,512]{3,2,1,0:T(8,128)(2,1)} collective-permute-done((bf16[4,1,256,512]{3,2,1,0:T(8,128)(2,1)}, bf16[4,1,256,512]{3,2,1,0:T(8,128)(2,1)}, u32[]{:S(2)}, u32[]{:S(2)}) %collective-permute-start.3) | collective-permute-done | bytes 1048608 | tf_op jit(solution)/shard_map/ppermute | solution.py:23
  81.8 55.3 %while.44 = (s32[]{:T(128)}, bf16[4,4,64,8,64]{4,2,3,1,0:T(8,128)(2,1)}, bf16[4,4,64,8,64]{4,3,2,1,0:T(8,128)(2,1)}, bf16[4,4,8,8,8]{3,4,2,1,0:T(8,128)(2,1)S(1)...) while((s32[]{:T(128)}, bf16[4,4,64,8,64]{4,2,3,1,0:T(8,128)(2,1)}, ...), condition=%wide.region_2.3_spmd.clone, body=%wide.region_1.2_spmd.sunk.clone | while | flops 152044640 | bytes 27333516 | solution.py:55
  85.1 3.6 reshape.475
  88.7 3.6 convert_bitcast_fusion.12
  98.9 3.6 reshape.475
  102.5 3.6 convert_bitcast_fusion.12
  112.8 3.6 reshape.475
  116.4 3.6 convert_bitcast_fusion.12
  126.6 3.6 reshape.475
  130.2 3.6 convert_bitcast_fusion.12
  142.0 55.1 %while.45 = (s32[]{:T(128)}, bf16[4,4,64,8,64]{4,2,3,1,0:T(8,128)(2,1)}, bf16[4,4,64,8,64]{4,2,3,1,0:T(8,128)(2,1)}, bf16[4,4,8,8,8]{3,4,2,1,0:T(8,128)(2,1)S(1)...) while((s32[]{:T(128)}, bf16[4,4,64,8,64]{4,2,3,1,0:T(8,128)(2,1)}, ...), condition=%wide.region_4.5_spmd.clone, body=%wide.region_3.4_spmd.sunk.clone | while | flops 152044640 | bytes 26810244 | solution.py:55
  145.3 3.6 reshape.479
  148.9 3.6 convert_bitcast_fusion.13
  159.0 3.6 reshape.479
  162.6 3.6 convert_bitcast_fusion.13
  172.8 3.6 reshape.479
  176.4 3.6 convert_bitcast_fusion.13
  186.6 3.6 reshape.479
  190.2 3.6 convert_bitcast_fusion.13
  223.1 22.8 %collective-permute-done.10 = bf16[4,1,256,512]{3,2,1,0:T(8,128)(2,1)} collective-permute-done((bf16[4,1,256,512]{3,2,1,0:T(8,128)(2,1)}, bf16[4,1,256,512]{3,2,1,0:T(8,128)(2,1)}, u32[]{:S(2)}, u32[]{:S(2)}) %collective-permute-start.10) | collective-permute-done | bytes 1048608 | tf_op jit(solution)/shard_map/ppermute | solution.py:21
  245.9 19.9 %collective-permute-done.11 = bf16[4,1,256,512]{3,2,1,0:T(8,128)(2,1)} collective-permute-done((bf16[4,1,256,512]{3,2,1,0:T(8,128)(2,1)}, bf16[4,1,256,512]{3,2,1,0:T(8,128)(2,1)}, u32[]{:S(2)}, u32[]{:S(2)}) %collective-permute-start.11) | collective-permute-done | bytes 1048608 | tf_op jit(solution)/shard_map/ppermute | solution.py:23
  270.9 52.9 %while.46 = (s32[]{:T(128)}, f32[4,4,64,8,64]{4,2,3,1,0:T(8,128)}, bf16[4,4,64,8,64]{4,2,3,1,0:T(8,128)(2,1)}, bf16[4,4,8,8,8]{3,4,2,1,0:T(8,128)(2,1)S(1)}, s32...) while((s32[]{:T(128)}, f32[4,4,64,8,64]{4,2,3,1,0:T(8,128)}, ...), condition=%wide.region_6.7_spmd.clone, body=%wide.region_5.6_spmd.sunk.clone | while | flops 152044640 | bytes 16324429 | solution.py:55
  274.1 3.6 reshape.483
  277.7 3.4 convert_bitcast_fusion.14
  287.4 3.6 reshape.483
  291.0 3.4 convert_bitcast_fusion.14
  300.6 3.6 reshape.483
  304.2 3.4 convert_bitcast_fusion.14
  313.8 3.6 reshape.483
  317.4 3.4 convert_bitcast_fusion.14
  326.4 5.2 %copy.32 = f32[4,4,64,8,64]{4,3,2,1,0:T(8,128)} copy(f32[4,4,64,8,64]{4,2,3,1,0:T(8,128)S(1)} %broadcast_multiply_fusion) | data formatting | bytes 4194304 | tf_op jit(solution)/shard_map/mul | solution.py:106
  331.6 4.8 %mul.63 = f32[1024,512]{1,0:T(8,128)} reshape(f32[4,4,64,8,64]{4,3,2,1,0:T(8,128)} %copy.32) | data formatting | bytes 4194304 | tf_op jit(solution)/shard_map/mul | solution.py:106
  340.4 4.8 %mul.66 = f32[2,2,256,512]{3,2,1,0:T(8,128)} reshape(f32[4,4,64,8,64]{4,3,2,1,0:T(8,128)} %copy.32) | data formatting | bytes 4194304 | tf_op jit(solution)/shard_map/mul | solution.py:106
  347.2 5.1 %collective-permute-done.12 = bf16[1,2,256,512]{3,2,1,0:T(8,128)(2,1)} collective-permute-done((bf16[1,2,256,512]{3,2,1,0:T(8,128)(2,1)}, bf16[1,2,256,512]{3,2,1,0:T(8,128)(2,1)}, u32[]{:S(2)}, u32[]{:S(2)}) %collective-permute-start.12) | collective-permute-done | bytes 524320 | tf_op jit(solution)/shard_map/ppermute | solution.py:21
  360.8 22.0 %collective-permute-done.14 = bf16[4,1,256,512]{3,2,1,0:T(8,128)(2,1)} collective-permute-done((bf16[4,1,256,512]{3,2,1,0:T(8,128)(2,1)}, bf16[4,1,256,512]{3,2,1,0:T(8,128)(2,1)}, u32[]{:S(2)}, u32[]{:S(2)}) %collective-permute-start.14) | collective-permute-done | bytes 1048608 | tf_op jit(solution)/shard_map/ppermute | solution.py:21
  382.8 17.8 %collective-permute-done.15 = bf16[4,1,256,512]{3,2,1,0:T(8,128)(2,1)} collective-permute-done((bf16[4,1,256,512]{3,2,1,0:T(8,128)(2,1)}, bf16[4,1,256,512]{3,2,1,0:T(8,128)(2,1)}, u32[]{:S(2)}, u32[]{:S(2)}) %collective-permute-start.15) | collective-permute-done | bytes 1048608 | tf_op jit(solution)/shard_map/ppermute | solution.py:23
  405.4 55.5 %while.47 = (s32[]{:T(128)}, f32[4,4,64,8,64]{4,3,2,1,0:T(8,128)}, bf16[4,4,64,8,64]{4,3,2,1,0:T(8,128)(2,1)}, bf16[4,4,8,8,8]{3,4,2,1,0:T(8,128)(2,1)S(1)}, s32...) while((s32[]{:T(128)}, f32[4,4,64,8,64]{4,3,2,1,0:T(8,128)}, ...), condition=%wide.region_8.9_spmd.clone, body=%wide.region_7.8_spmd.sunk.clone | while | flops 152044640 | bytes 17634640 | solution.py:55
  408.7 3.6 reshape.487
  412.3 3.4 convert_bitcast_fusion.15
  422.5 3.6 reshape.487
  426.1 3.4 convert_bitcast_fusion.15
  436.4 3.6 reshape.487
  440.0 3.4 convert_bitcast_fusion.15
  450.3 3.6 reshape.487
  453.9 3.4 convert_bitcast_fusion.15
  460.9 4.8 %reshape.368 = f32[1024,512]{1,0:T(8,128)} reshape(f32[4,4,64,8,64]{4,3,2,1,0:T(8,128)} %get-tuple-element.136) | data formatting | bytes 4194304 | tf_op jit(solution)/shard_map/reshape | solution.py:56
  (240 shorter events, 197.7 us)
Async XLA Ops:
  0.0 10.2 %copy-start.19 = (s32[4]{0:T(128)S(1)}, s32[4]{0:T(128)}, u32[]{:S(2)}) copy-start(s32[4]{0:T(128)} %constant.111.clone) | copy-start | bytes 52
  0.0 10.2 %copy-start.20 = (s32[4]{0:T(128)S(1)}, s32[4]{0:T(128)}, u32[]{:S(2)}) copy-start(s32[4]{0:T(128)} %constant.112.clone) | copy-start | bytes 52
  0.0 10.2 %copy-start.21 = (s32[4]{0:T(128)S(1)}, s32[4]{0:T(128)}, u32[]{:S(2)}) copy-start(s32[4]{0:T(128)} %constant.113) | copy-start | bytes 52
  0.0 26.3 %copy-start.6 = (bf16[1024,512]{1,0:T(8,128)(2,1)S(1)}, bf16[1024,512]{1,0:T(8,128)(2,1)}, u32[]{:S(2)}) copy-start(bf16[1024,512]{1,0:T(8,128)(2,1)} %param.15) | copy-start | bytes 3145732
  0.0 10.6 %copy-start.18 = (s32[512,8]{0,1:T(8,128)S(1)}, s32[512,8]{0,1:T(8,128)}, u32[]{:S(2)}) copy-start(s32[512,8]{0,1:T(8,128)} %param.17) | copy-start | bytes 49156
  2.4 20.3 %collective-permute-start = (bf16[1,2,256,512]{3,2,1,0:T(8,128)(2,1)}, bf16[1,2,256,512]{3,2,1,0:T(8,128)(2,1)S(1)}, u32[]{:S(2)}, u32[]{:S(2)}) collective-permute-start(bf16[1,2,256,512]{3,2,1,0:T(8,128)(2,1)} %bitcast.50), channel_id=1, source_target_pairs={{0,2},{2,4},{4,6},{6,8},{8,10},{10,12},{12,14},{14,16},{16,18},{18... | collective-permute-start | bytes 1572872 | tf_op jit(solution)/shard_map/ppermute | solution.py:21
  5.0 20.5 %collective-permute-start.1 = (bf16[1,2,256,512]{3,2,1,0:T(8,128)(2,1)}, bf16[1,2,256,512]{3,2,1,0:T(8,128)(2,1)S(1)}, u32[]{:S(2)}, u32[]{:S(2)}) collective-permute-start(bf16[1,2,256,512]{3,2,1,0:T(8,128)(2,1)} %bitcast.52), channel_id=1, source_target_pairs={{2,0},{4,2},{6,4},{8,6},{10,8},{12,10},{14,12},{16,14},{18,16},{20... | collective-permute-start | bytes 1572872 | tf_op jit(solution)/shard_map/ppermute | solution.py:23
  7.3 30.4 %collective-permute-start.4 = (bf16[1,2,256,512]{3,2,1,0:T(8,128)(2,1)}, bf16[1,2,256,512]{3,2,1,0:T(8,128)(2,1)S(1)}, u32[]{:S(2)}, u32[]{:S(2)}) collective-permute-start(bf16[1,2,256,512]{3,2,1,0:T(8,128)(2,1)} %bitcast.55), channel_id=1, source_target_pairs={{0,2},{2,4},{4,6},{6,8},{8,10},{10,12},{12,14},{14,16},{16,18},{18... | collective-permute-start | bytes 1572872 | tf_op jit(solution)/shard_map/ppermute | solution.py:21
  9.0 28.6 %collective-permute-start.5 = (bf16[1,2,256,512]{3,2,1,0:T(8,128)(2,1)}, bf16[1,2,256,512]{3,2,1,0:T(8,128)(2,1)}, u32[]{:S(2)}, u32[]{:S(2)}) collective-permute-start(bf16[1,2,256,512]{3,2,1,0:T(8,128)(2,1)} %bitcast.57), channel_id=1, source_target_pairs={{2,0},{4,2},{6,4},{8,6},{10,8},{12,10},{14,12},{16,14},{18,16},{20... | collective-permute-start | bytes 1572872 | tf_op jit(solution)/shard_map/ppermute | solution.py:23
  22.7 2.8 copy-start.13
  26.3 4.5 copy-start.4
  29.3 25.6 %collective-permute-start.2 = (bf16[4,1,256,512]{3,2,1,0:T(8,128)(2,1)}, bf16[4,1,256,512]{3,2,1,0:T(8,128)(2,1)}, u32[]{:S(2)}, u32[]{:S(2)}) collective-permute-start(bf16[4,1,256,512]{3,2,1,0:T(8,128)(2,1)} %get-tuple-element.222), channel_id=1, source_target_pairs={{0,1},{1,0},{2,3},{3,2},{4,5},{5,4},{6,7},{7,6},{8,9},{9,8},{10,11... | collective-permute-start | bytes 3145736 | tf_op jit(solution)/shard_map/ppermute | solution.py:21
  30.5 46.8 %collective-permute-start.3 = (bf16[4,1,256,512]{3,2,1,0:T(8,128)(2,1)}, bf16[4,1,256,512]{3,2,1,0:T(8,128)(2,1)}, u32[]{:S(2)}, u32[]{:S(2)}) collective-permute-start(bf16[4,1,256,512]{3,2,1,0:T(8,128)(2,1)} %get-tuple-element.223), channel_id=1, source_target_pairs={{1,0},{0,1},{3,2},{2,3},{5,4},{4,5},{7,6},{6,7},{9,8},{8,9},{11,10... | collective-permute-start | bytes 3145736 | tf_op jit(solution)/shard_map/ppermute | solution.py:23
  34.1 1.3 copy-start
  37.7 3.0 copy-start.12
  37.7 39.6 %copy-start.14 = (bf16[1,2,256,512]{3,2,1,0:T(8,128)(2,1)S(1)}, bf16[1,2,256,512]{3,2,1,0:T(8,128)(2,1)}, u32[]{:S(2)}) copy-start(bf16[1,2,256,512]{3,2,1,0:T(8,128)(2,1)} %copy-done.13) | copy-start | bytes 1572868
  37.7 39.6 %copy-start.16 = (bf16[1,2,256,512]{3,2,1,0:T(8,128)(2,1)S(1)}, bf16[1,2,256,512]{3,2,1,0:T(8,128)(2,1)}, u32[]{:S(2)}) copy-start(bf16[1,2,256,512]{3,2,1,0:T(8,128)(2,1)} %copy-done.15) | copy-start | bytes 1572868
  40.7 96.5 %collective-permute-start.6 = (bf16[4,1,256,512]{3,2,1,0:T(8,128)(2,1)}, bf16[4,1,256,512]{3,2,1,0:T(8,128)(2,1)}, u32[]{:S(2)}, u32[]{:S(2)}) collective-permute-start(bf16[4,1,256,512]{3,2,1,0:T(8,128)(2,1)} %get-tuple-element.220), channel_id=1, source_target_pairs={{0,1},{1,0},{2,3},{3,2},{4,5},{5,4},{6,7},{7,6},{8,9},{9,8},{10,11... | collective-permute-start | bytes 3145736 | tf_op jit(solution)/shard_map/ppermute | solution.py:21
  41.9 95.3 %collective-permute-start.7 = (bf16[4,1,256,512]{3,2,1,0:T(8,128)(2,1)}, bf16[4,1,256,512]{3,2,1,0:T(8,128)(2,1)}, u32[]{:S(2)}, u32[]{:S(2)}) collective-permute-start(bf16[4,1,256,512]{3,2,1,0:T(8,128)(2,1)} %get-tuple-element.221), channel_id=1, source_target_pairs={{1,0},{0,1},{3,2},{2,3},{5,4},{4,5},{7,6},{6,7},{9,8},{8,9},{11,10... | collective-permute-start | bytes 3145736 | tf_op jit(solution)/shard_map/ppermute | solution.py:23
  88.7 4.7 %copy-start.10 = (bf16[4,4,64,8,64]{4,2,3,1,0:T(8,128)(2,1)S(1)}, bf16[4,4,64,8,64]{4,2,3,1,0:T(8,128)(2,1)}, u32[]{:S(2)}) copy-start(bf16[4,4,64,8,64]{4,2,3,1,0:T(8,128)(2,1)} %get-tuple-element.445) | copy-start | bytes 3145732 | tf_op jit(solution)/shard_map/while
  94.3 1.3 copy-start.11
  102.5 4.7 %copy-start.10 = (bf16[4,4,64,8,64]{4,2,3,1,0:T(8,128)(2,1)S(1)}, bf16[4,4,64,8,64]{4,2,3,1,0:T(8,128)(2,1)}, u32[]{:S(2)}) copy-start(bf16[4,4,64,8,64]{4,2,3,1,0:T(8,128)(2,1)} %get-tuple-element.445) | copy-start | bytes 3145732 | tf_op jit(solution)/shard_map/while
  108.2 1.3 copy-start.11
  116.4 4.7 %copy-start.10 = (bf16[4,4,64,8,64]{4,2,3,1,0:T(8,128)(2,1)S(1)}, bf16[4,4,64,8,64]{4,2,3,1,0:T(8,128)(2,1)}, u32[]{:S(2)}) copy-start(bf16[4,4,64,8,64]{4,2,3,1,0:T(8,128)(2,1)} %get-tuple-element.445) | copy-start | bytes 3145732 | tf_op jit(solution)/shard_map/while
  122.0 1.3 copy-start.11
  130.2 4.7 %copy-start.10 = (bf16[4,4,64,8,64]{4,2,3,1,0:T(8,128)(2,1)S(1)}, bf16[4,4,64,8,64]{4,2,3,1,0:T(8,128)(2,1)}, u32[]{:S(2)}) copy-start(bf16[4,4,64,8,64]{4,2,3,1,0:T(8,128)(2,1)} %get-tuple-element.445) | copy-start | bytes 3145732 | tf_op jit(solution)/shard_map/while
  135.8 1.3 copy-start.11
  148.9 3.6 copy-start.1
  154.4 1.3 copy-start.2
  162.6 3.6 copy-start.1
  168.2 1.3 copy-start.2
  176.4 3.6 copy-start.1
  182.0 1.3 copy-start.2
  190.2 3.6 copy-start.1
  195.8 1.3 copy-start.2
  199.8 6.7 %copy-start.3 = (bf16[4,4,64,8,64]{4,2,3,1,0:T(8,128)(2,1)S(1)}, bf16[4,4,64,8,64]{4,2,3,1,0:T(8,128)(2,1)}, u32[]{:S(2)}) copy-start(bf16[4,4,64,8,64]{4,2,3,1,0:T(8,128)(2,1)} %get-tuple-element.134) | copy-start | bytes 3145732
  201.9 13.3 %collective-permute-start.8 = (bf16[1,2,256,512]{3,2,1,0:T(8,128)(2,1)}, bf16[1,2,256,512]{3,2,1,0:T(8,128)(2,1)}, u32[]{:S(2)}, u32[]{:S(2)}) collective-permute-start(bf16[1,2,256,512]{3,2,1,0:T(8,128)(2,1)} %slice.87), channel_id=1, source_target_pairs={{0,2},{2,4},{4,6},{6,8},{8,10},{10,12},{12,14},{14,16},{16,18},{18... | collective-permute-start | bytes 1572872 | tf_op jit(solution)/shard_map/ppermute | solution.py:21
  206.5 9.9 %collective-permute-start.9 = (bf16[1,2,256,512]{3,2,1,0:T(8,128)(2,1)}, bf16[1,2,256,512]{3,2,1,0:T(8,128)(2,1)}, u32[]{:S(2)}, u32[]{:S(2)}) collective-permute-start(bf16[1,2,256,512]{3,2,1,0:T(8,128)(2,1)} %slice.89), channel_id=1, source_target_pairs={{2,0},{4,2},{6,4},{8,6},{10,8},{12,10},{14,12},{16,14},{18,16},{20... | collective-permute-start | bytes 1572872 | tf_op jit(solution)/shard_map/ppermute | solution.py:23
  212.8 7.5 %copy-start.8 = (bf16[2,2,256,512]{3,2,1,0:T(8,128)(2,1)}, bf16[2,2,256,512]{3,2,1,0:T(8,128)(2,1)S(1)}, u32[]{:S(2)}) copy-start(bf16[2,2,256,512]{3,2,1,0:T(8,128)(2,1)S(1)} %convert_element_type.60) | copy-start | bytes 3145732
  212.8 9.0 %copy-start.5 = (bf16[4,4,64,8,64]{4,3,2,1,0:T(8,128)(2,1)S(1)}, bf16[4,4,64,8,64]{4,3,2,1,0:T(8,128)(2,1)}, u32[]{:S(2)}) copy-start(bf16[4,4,64,8,64]{4,3,2,1,0:T(8,128)(2,1)} %copy.28) | copy-start | bytes 3145732
  220.4 25.6 %collective-permute-start.10 = (bf16[4,1,256,512]{3,2,1,0:T(8,128)(2,1)}, bf16[4,1,256,512]{3,2,1,0:T(8,128)(2,1)}, u32[]{:S(2)}, u32[]{:S(2)}) collective-permute-start(bf16[4,1,256,512]{3,2,1,0:T(8,128)(2,1)} %get-tuple-element.216), channel_id=1, source_target_pairs={{0,1},{1,0},{2,3},{3,2},{4,5},{5,4},{6,7},{7,6},{8,9},{9,8},{10,11... | collective-permute-start | bytes 3145736 | tf_op jit(solution)/shard_map/ppermute | solution.py:21
  221.6 44.2 %collective-permute-start.11 = (bf16[4,1,256,512]{3,2,1,0:T(8,128)(2,1)}, bf16[4,1,256,512]{3,2,1,0:T(8,128)(2,1)}, u32[]{:S(2)}, u32[]{:S(2)}) collective-permute-start(bf16[4,1,256,512]{3,2,1,0:T(8,128)(2,1)} %get-tuple-element.217), channel_id=1, source_target_pairs={{1,0},{0,1},{3,2},{2,3},{5,4},{4,5},{7,6},{6,7},{9,8},{8,9},{11,10... | collective-permute-start | bytes 3145736 | tf_op jit(solution)/shard_map/ppermute | solution.py:23
  338.4 6.8 %copy-start.9 = (bf16[2,2,256,512]{3,2,1,0:T(8,128)(2,1)S(1)}, bf16[2,2,256,512]{3,2,1,0:T(8,128)(2,1)}, u32[]{:S(2)}) copy-start(bf16[2,2,256,512]{3,2,1,0:T(8,128)(2,1)} %copy-done.8) | copy-start | bytes 3145732
  339.4 12.8 %collective-permute-start.12 = (bf16[1,2,256,512]{3,2,1,0:T(8,128)(2,1)}, bf16[1,2,256,512]{3,2,1,0:T(8,128)(2,1)}, u32[]{:S(2)}, u32[]{:S(2)}) collective-permute-start(bf16[1,2,256,512]{3,2,1,0:T(8,128)(2,1)} %bitcast.62), channel_id=1, source_target_pairs={{0,2},{2,4},{4,6},{6,8},{8,10},{10,12},{12,14},{14,16},{16,18},{18... | collective-permute-start | bytes 1572872 | tf_op jit(solution)/shard_map/ppermute | solution.py:21
  340.4 13.9 %collective-permute-start.13 = (bf16[1,2,256,512]{3,2,1,0:T(8,128)(2,1)}, bf16[1,2,256,512]{3,2,1,0:T(8,128)(2,1)}, u32[]{:S(2)}, u32[]{:S(2)}) collective-permute-start(bf16[1,2,256,512]{3,2,1,0:T(8,128)(2,1)} %bitcast.63), channel_id=1, source_target_pairs={{2,0},{4,2},{6,4},{8,6},{10,8},{12,10},{14,12},{16,14},{18,16},{20... | collective-permute-start | bytes 1572872 | tf_op jit(solution)/shard_map/ppermute | solution.py:23
  347.2 11.6 %copy-start.17 = (bf16[1024,512]{1,0:T(8,128)(2,1)S(1)}, bf16[1024,512]{1,0:T(8,128)(2,1)}, u32[]{:S(2)}) copy-start(bf16[1024,512]{1,0:T(8,128)(2,1)} %param.16) | copy-start | bytes 3145732
  357.3 25.6 %collective-permute-start.14 = (bf16[4,1,256,512]{3,2,1,0:T(8,128)(2,1)}, bf16[4,1,256,512]{3,2,1,0:T(8,128)(2,1)}, u32[]{:S(2)}, u32[]{:S(2)}) collective-permute-start(bf16[4,1,256,512]{3,2,1,0:T(8,128)(2,1)} %get-tuple-element.214), channel_id=1, source_target_pairs={{0,1},{1,0},{2,3},{3,2},{4,5},{5,4},{6,7},{7,6},{8,9},{9,8},{10,11... | collective-permute-start | bytes 3145736 | tf_op jit(solution)/shard_map/ppermute | solution.py:21
  358.5 42.1 %collective-permute-start.15 = (bf16[4,1,256,512]{3,2,1,0:T(8,128)(2,1)}, bf16[4,1,256,512]{3,2,1,0:T(8,128)(2,1)}, u32[]{:S(2)}, u32[]{:S(2)}) collective-permute-start(bf16[4,1,256,512]{3,2,1,0:T(8,128)(2,1)} %get-tuple-element.215), channel_id=1, source_target_pairs={{1,0},{0,1},{3,2},{2,3},{5,4},{4,5},{7,6},{6,7},{9,8},{8,9},{11,10... | collective-permute-start | bytes 3145736 | tf_op jit(solution)/shard_map/ppermute | solution.py:23
  (2 other events, 2.1 us)
where the time goes:
time: 468 us; the launch traced here: 466 us
  local copies, waits for them, and re-layouts  195 us (42%)
  waiting for transfers between devices  141 us (30%)
  matrix products  82.9 us (18%)
  other arithmetic  31.9 us (7%)
  starting transfers between devices  13.6 us (3%)
    ppermute x8, waiting for transfers between devices, extended_2(): lax.ppermute(tail, axis, [(i, (i + 1) % count) for i in range(count)])  76.5 us
    ppermute x8, waiting for transfers between devices, extended_2(): lax.ppermute(head, axis, [((i + 1) % count, i) for i in range(count)])  64.9 us
    reshape x16, local copies, waits for them, and re-layouts, product_rows(): far_rows = extended[place_rows].reshape(group, NB, BS, NB, BS)  57.6 us
    dot_general x16, matrix products, product_rows(): jnp.einsum('iasct,iacb->iasbt', far_rows, map_rows, preferred_element_typ...  55.8 us
    gather x16, local copies, waits for them, and re-layouts, product_rows(): far_rows = extended[place_rows].reshape(group, NB, BS, NB, BS)  50.7 us
    dot_general x16, matrix products, product_rows(): jnp.einsum('iras,iasbt->irbt', left_rows, moved, preferred_element_type=j...  27 us
    mul x3, local copies, waits for them, and re-layouts, body(): 2.0 * fifth  14.8 us
    slice x9, local copies, waits for them, and re-layouts, extended_2(): lax.slice_in_dim(cells, cells.shape[dim] - width, cells.shape[dim], axis=...  13.8 us
  transfers between devices with their start and end apart: 16, of which 11 were waited for; matrix products, arithmetic and copies ran while one was open for 19% of the time, Pallas kernels for 0%

commit v1 on v0

v1 whole, which is shorter than its diff:
```python
import functools

import jax
import jax.numpy as jnp
import numpy as np
from jax import lax
from jax.experimental import pallas as pl
from jax.experimental.pallas import tpu as pltpu
from jax.sharding import PartitionSpec as P

BS = 64
NB = 8
EDGE = 4
BLK_DEV = 16
OWN = BLK_DEV * NB
DIRS = ((0, -1), (0, 1), (-1, 0), (1, 0), (-1, -1), (-1, 1), (1, -1), (1, 1))
CORNERS = {-1: (1,), 0: (0, 1), 1: (0,)}


def direction_rows(s, t):
    return [EDGE * (2 * p + q) + r for p in CORNERS[s] for q in CORNERS[t] for r in range(EDGE)]


ROWS = [direction_rows(s, t) for s, t in DIRS]
FULL = tuple(len(rows) * NB for rows in ROWS)
SMALL = (32, 32, 24, 24, 16, 16, 16, 16)
GHOST = sum(FULL)
STARTS = np.cumsum((0,) + FULL)
WIDEST = max(FULL)


def starts_of(caps):
    return [int(v) for v in np.cumsum((0,) + caps)]


def tables(columns, along_gx, along_gy, gx_index, gy_index):
    count = along_gx * along_gy
    ids = jnp.arange(count * BLK_DEV, dtype=jnp.int32).reshape(along_gx, along_gy, BLK_DEV)
    slots = columns.reshape(along_gx, along_gy, BLK_DEV, NB)
    ghost_ids, ghost_slots = [], []
    for (s, t), rows in zip(DIRS, ROWS):
        for source, kept in ((ids[..., None], ghost_ids), (slots, ghost_slots)):
            moved = jnp.roll(source, (-s, -t), (0, 1))
            pieces = [moved[:, :, r : r + EDGE] for r in rows[::EDGE]]
            kept.append(jnp.concatenate(pieces, axis=2))
    ghost_slots = jnp.concatenate(ghost_slots, axis=2).reshape(count, GHOST)
    ghost_ids = jnp.concatenate(ghost_ids, axis=2)
    ghost_ids = jnp.broadcast_to(ghost_ids, ghost_ids.shape[:3] + (NB,)).reshape(count, GHOST)
    live = jnp.where(slots >= 0, slots, -2).reshape(count, BLK_DEV, NB)
    names_row = jnp.zeros((count, BLK_DEV, GHOST), bool)
    names_column = jnp.zeros((count, BLK_DEV, GHOST), bool)
    for b in range(NB):
        names_row |= live[:, :, b, None] == ghost_ids[:, None, :]
        names_column |= live[:, :, b, None] == ghost_slots[:, None, :]
    need = jnp.any(names_row & names_column, axis=1)
    segment = np.repeat(np.arange(len(DIRS)), FULL)
    before = (segment[:, None] == segment[None, :]) & (np.arange(GHOST)[:, None] < np.arange(GHOST)[None, :])
    ones = need.astype(jnp.bfloat16)
    rank = jnp.dot(ones, jnp.asarray(before, jnp.bfloat16), preferred_element_type=jnp.float32).astype(jnp.int32)
    limit = jnp.asarray(np.repeat(SMALL, FULL).astype(np.int32))
    fits = jnp.all(jnp.where(need, rank < limit, True))
    ranked = jnp.where(need, rank, -1)

    own_rank = lax.dynamic_index_in_dim(ranked, gx_index * along_gy + gy_index, 0, keepdims=False)
    by_device = ranked.reshape(along_gx, along_gy, GHOST)
    sent_rank = jnp.concatenate(
        [jnp.roll(by_device[:, :, lo:hi], (s, t), (0, 1)) for (s, t), lo, hi in zip(DIRS, STARTS[:-1], STARTS[1:])],
        axis=2,
    ).reshape(count, GHOST)
    sent_rank = lax.dynamic_index_in_dim(sent_rank, gx_index * along_gy + gy_index, 0, keepdims=False)
    block = np.concatenate([[1 + r * NB + c for r in rows for c in range(NB)] for rows in ROWS])
    chosen = (sent_rank[:, None] == jnp.arange(WIDEST, dtype=jnp.int32)[None, :]).astype(jnp.bfloat16)
    weights = (segment[None, :] == np.arange(len(DIRS))[:, None]) * block[None, :]
    sends = jnp.dot(jnp.asarray(weights, jnp.bfloat16), chosen, preferred_element_type=jnp.float32)
    sends = sends.astype(jnp.int32)

    me = gx_index * along_gy + gy_index
    own_slots = lax.dynamic_index_in_dim(columns.reshape(count, BLK_DEV, NB), me, 0, keepdims=False)
    my_ghost_slots = lax.dynamic_index_in_dim(ghost_slots, me, 0, keepdims=False)
    my_ghost_ids = lax.dynamic_index_in_dim(ghost_ids, me, 0, keepdims=False)
    flat_slots = jnp.concatenate([own_slots.reshape(-1), my_ghost_slots])
    row_ids = jnp.concatenate([jnp.repeat(me * BLK_DEV + jnp.arange(BLK_DEV, dtype=jnp.int32), NB), my_ghost_ids])
    wanted = jnp.where(own_slots >= 0, own_slots, -2)
    of_row = wanted[:, :, None] == row_ids[None, None, :]
    of_column = wanted[:, :, None] == flat_slots[None, None, :]

    def places(caps):
        offset = np.repeat(starts_of(caps)[:-1], FULL) + 1 + OWN
        ghost = jnp.where(own_rank >= 0, own_rank + jnp.asarray(offset, jnp.int32), 0)
        place = jnp.concatenate([1 + jnp.arange(OWN, dtype=jnp.int32), ghost])
        both = of_row[:, :, None, :] & of_column[:, None, :, :]
        return jnp.sum(jnp.where(both, place[None, None, None, :], 0), axis=3).reshape(-1)

    def send_list(caps):
        return jnp.concatenate([sends[d, :cap] for d, cap in enumerate(caps)])

    return fits, places, send_list


def purify(sizes, caps, place_ref, send_ref, kernel_ref, margin_ref, ham_ref, out_ref,
           blocks, other, lead, cubic, out_box, in_box, send_sem, recv_sem):
    along_gx, along_gy = sizes
    pair_starts = [v // 2 for v in starts_of(caps)]
    pairs = pair_starts[-1]
    gx_index, gy_index = lax.axis_index("gx"), lax.axis_index("gy")
    targets = [
        (lax.rem(gx_index - s + along_gx, along_gx), lax.rem(gy_index - t + along_gy, along_gy)) for s, t in DIRS
    ]
    low = lax.broadcasted_iota(jnp.int32, (BS, 2 * BS), 1) < BS

    def own(source, into):
        @pl.loop(0, BLK_DEV)
        def _(i):
            rows = pl.ds(pl.multiple_of(i * BS, BS), BS)
            for c in range(NB):
                block = source[rows, c * BS : (c + 1) * BS]
                into[1 + i * NB + c] = jnp.concatenate([block, block], axis=1)

    def exchange(turn, source):
        slot = turn % 2

        @pl.loop(0, pairs // 2)
        def _(h):
            for j in range(2):
                first = source[send_ref[4 * h + 2 * j]]
                second = source[send_ref[4 * h + 2 * j + 1]]
                out_box[slot, 2 * h + j] = jnp.where(low, first, second)

        copies = []
        for d, target in enumerate(targets):
            part = pl.ds(pair_starts[d], pair_starts[d + 1] - pair_starts[d])
            copies.append(
                pltpu.make_async_remote_copy(
                    src_ref=out_box.at[slot, part],
                    dst_ref=in_box.at[turn, part],
                    send_sem=send_sem.at[turn, d],
                    recv_sem=recv_sem.at[turn, d],
                    device_id=target,
                    device_id_type=pl.DeviceIdType.MESH,
                )
            )
        return copies

    def arrive(turn, copies, into):
        for copy in copies:
            copy.wait_recv()

        @pl.loop(0, pairs // 2)
        def _(h):
            for j in range(2):
                pair = in_box[turn, 2 * h + j]
                first, second = pair[:, :BS], pair[:, BS:]
                at = 1 + OWN + 4 * h + 2 * j
                into[at] = jnp.concatenate([first, first], axis=1)
                into[at + 1] = jnp.concatenate([second, second], axis=1)

    def product(left, right, finish):
        @pl.loop(0, BLK_DEV)
        def _(i):
            rows = pl.ds(pl.multiple_of(i * BS, BS), BS)
            left_rows = left[rows, :]
            for half in range(2):
                wide = []
                for b in (4 * half, 4 * half + 2):
                    tall = []
                    for a in range(NB):
                        at = (i * NB + a) * NB + b
                        tall.append(jnp.where(low, right[place_ref[at]], right[place_ref[at + 1]]))
                    wide.append(jnp.concatenate(tall, axis=0))
                result = jnp.dot(left_rows, jnp.concatenate(wide, axis=1), preferred_element_type=jnp.float32)
                finish(rows, slice(4 * half * BS, 4 * (half + 1) * BS), result)

    def put_lead(rows, cols, result):
        lead[rows, cols] = result.astype(jnp.bfloat16)

    def put_cubic(rows, cols, result):
        cubic[rows, cols] = result.astype(jnp.bfloat16)

    def put_purified(rows, cols, result):
        value = 3.0 * cubic[rows, cols].astype(jnp.float32) - 2.0 * result
        cubic[rows, cols] = value.astype(jnp.bfloat16)

    def put_out(rows, cols, result):
        out_ref[rows, cols] = result

    barrier = pltpu.get_barrier_semaphore()
    for target, (s, t) in zip(targets, DIRS):
        pl.semaphore_signal(barrier, inc=1, device_id=target, device_id_type=pl.DeviceIdType.MESH)
    zero = jnp.zeros((BS, 2 * BS), jnp.bfloat16)
    blocks[0] = zero
    other[0] = zero
    own(margin_ref, blocks)
    first = exchange(0, blocks)
    pl.semaphore_wait(barrier, len(DIRS))
    for copy in first:
        copy.start()
    own(kernel_ref, other)
    second = exchange(1, other)
    for copy in second:
        copy.start()
    arrive(0, first, blocks)
    product(kernel_ref, blocks, put_lead)
    arrive(1, second, other)
    product(lead, other, put_cubic)
    own(cubic, blocks)
    for copy in first:
        copy.wait_send()
    third = exchange(2, blocks)
    for copy in third:
        copy.start()
    arrive(2, third, blocks)
    product(lead, blocks, put_purified)
    own(cubic, other)
    for copy in second:
        copy.wait_send()
    fourth = exchange(3, other)
    for copy in fourth:
        copy.start()
    arrive(3, fourth, other)
    product(ham_ref, other, put_out)
    for copy in third + fourth:
        copy.wait_send()


def call(sizes, caps, collective_id, places, send_list, kernel, margin, hamiltonian):
    pairs = sum(caps) // 2
    rows, width = kernel.shape
    in_vmem = pl.BlockSpec(memory_space=pltpu.VMEM)
    in_smem = pl.BlockSpec(memory_space=pltpu.SMEM)
    block_count = 1 + OWN + sum(caps)
    return pl.pallas_call(
        functools.partial(purify, sizes, caps),
        out_shape=jax.ShapeDtypeStruct((rows, width), jnp.float32),
        in_specs=[in_smem, in_smem, in_vmem, in_vmem, in_vmem],
        out_specs=in_vmem,
        scratch_shapes=[
            pltpu.VMEM((block_count, BS, 2 * BS), jnp.bfloat16),
            pltpu.VMEM((block_count, BS, 2 * BS), jnp.bfloat16),
            pltpu.VMEM((rows, width), jnp.bfloat16),
            pltpu.VMEM((rows, width), jnp.bfloat16),
            pltpu.VMEM((2, pairs, BS, 2 * BS), jnp.bfloat16),
            pltpu.VMEM((4, pairs, BS, 2 * BS), jnp.bfloat16),
            pltpu.SemaphoreType.DMA((4, len(DIRS))),
            pltpu.SemaphoreType.DMA((4, len(DIRS))),
        ],
        compiler_params=pltpu.CompilerParams(
            collective_id=collective_id, has_side_effects=True, vmem_limit_bytes=56 * 2**20
        ),
    )(places, send_list, kernel, margin, hamiltonian)


def body(sizes, kernel, margin, hamiltonian, columns):
    fits, places, send_list = tables(columns, *sizes, lax.axis_index("gx"), lax.axis_index("gy"))

    def run(caps, collective_id):
        return lambda: call(
            sizes, caps, collective_id, places(caps), send_list(caps), kernel, margin, hamiltonian
        )

    return lax.cond(fits, run(SMALL, 0), run(FULL, 1))


def solution(mesh):
    sizes = (mesh.shape["gx"], mesh.shape["gy"])
    in_specs = (P(("gx", "gy"), None), P(("gx", "gy"), None), P(("gx", "gy"), None), P())
    out_specs = P(("gx", "gy"), None)
    return jax.shard_map(
        functools.partial(body, sizes), mesh=mesh, in_specs=in_specs, out_specs=out_specs, check_vma=False
    )
```

time: 468 us -> 153 us (0.33)
  local copies, waits for them, and re-layouts: 195 us -> 14.5 us
  waiting for transfers between devices: 141 us -> 0 us
  Pallas kernels: 0 us -> 127 us
  matrix products: 82.9 us -> 1.04 us
  other arithmetic: 31.9 us -> 8.1 us
  starting transfers between devices: 13.6 us -> 0 us
    ppermute x16 -> x0, waiting for transfers between devices: 141 us -> none  [the longest x8 76.5 us: extended_2(): lax.ppermute(tail, axis, [(i, (i + 1) % count) for i in range(count)])]
    pallas_call x0 -> x1, Pallas kernels: none -> 127 us  [call(): pl.pallas_call(functools.partial(purify, sizes, caps), out_shape=jax.Shap...]
    dot_general x32 -> x2, matrix products: 82.9 us -> 1.04 us  [the longest x1 0.81 us: tables(): jnp.dot(ones, jnp.asarray(before, jnp.bfloat16), preferred_element_type=j...]
    reshape x19 -> x7, local copies, waits for them, and re-layouts: 66.4 us -> 2.66 us  [the longest x2 1.74 us: tables(): slots = columns.reshape(along_gx, along_gy, BLK_DEV, NB)]
    gather x18 -> x0, local copies, waits for them, and re-layouts: 51.9 us -> none  [the longest x16 50.7 us: product_rows(): far_rows = extended[place_rows].reshape(group, NB, BS, NB, BS)]
    concatenate x13 -> x25, other arithmetic: 23.8 us -> 3.06 us  [the longest x10 2.82 us: tables(): moved = jnp.roll(source, (-s, -t), (0, 1))]
    slice x12 -> x15, local copies, waits for them, and re-layouts: 19.8 us -> 2.62 us  [the longest x10 2.2 us: tables(): moved = jnp.roll(source, (-s, -t), (0, 1))]
    mul x3 -> x0, local copies, waits for them, and re-layouts: 14.8 us -> none  [body(): 2.0 * fifth]
  transfers between devices with their start and end apart: 16 -> 0, of which waited for: 11 -> 0; matrix products, arithmetic and copies ran while one was open for 19% -> 0% of each run, Pallas kernels for 0% -> 0%
where the time goes in v1:
time: 153 us; the launch traced here: 152 us
  Pallas kernels  127 us (83%)
  local copies, waits for them, and re-layouts  14.5 us (9%)
  other arithmetic  8.1 us (5%)
    pallas_call x1, Pallas kernels, call(): pl.pallas_call(functools.partial(purify, sizes, caps), out_shape=jax.Shap...  127 us
    concatenate x2, local copies, waits for them, and re-layouts, tables(): ghost_slots = jnp.concatenate(ghost_slots, axis=2).reshape(count, GHOST)  5.31 us

profile of v1, /device:TPU:1, one launch (start us, length us, event | category | flops | bytes accessed | tf_op | source)
XLA Modules:
  0.0 152.3 jit_solution(14607242454142578565)
XLA Ops:
  0.0 0.1 broadcast_in_dim.67
  0.1 0.1 reshape.85
  0.2 0.8 fusion.30
  0.9 0.1 slice.458
  1.0 0.1 slice.451
  1.2 0.1 fusion.12
  1.3 0.1 pad_add_fusion.7
  1.4 0.1 pad_add_fusion.8
  1.5 0.9 fusion.29
  2.4 0.2 pad_add_fusion.9
  2.6 0.3 concatenate.150
  2.9 0.1 slice.456
  3.0 0.1 slice.453
  3.1 0.8 reshape.83
  4.0 0.1 copy.51
  4.1 0.1 copy.52
  4.2 0.1 reshape.86
  4.3 0.9 reshape.84
  5.2 0.1 fusion.20
  5.3 0.1 fusion.8
  5.4 0.2 fusion.4
  5.6 0.1 fusion.7
  5.7 0.9 pad_add_fusion.2
  6.7 0.9 pad_add_fusion.4
  7.6 5.0 %concatenate.156 = s32[16,2,48,8]{2,1,0,3:T(2,128)S(1)} concatenate(s32[16,2,4,8]{2,1,0,3:T(2,128)S(1)} %get-tuple-element.122, s32[16,2,4,8]{2,1,0,3:T(2,128)S(1)} %get-tuple-element.123, s32[16,2,4,8]{2,1,0,3:T(2,128)S(1)} %get-tuple-element.124, s32[16,2,4,8]{2,1,0,3:T(2,128)S(1)} %get-tuple-element.121, s32[16,2,8,8]{2,1,0,3:T(2,128)S(1)} %get-tuple-element.178, ...), dimensions={2} | concatenate | bytes 98304 | tf_op jit(solution)/shard_map/concatenate | solution.py:46
  12.7 0.0 copy-start.1
  12.7 0.0 copy-start.2
  12.7 0.3 copy.50
  13.0 0.4 eq.116
  13.4 0.3 broadcast_in_dim.64
  13.7 0.4 eq.92
  14.1 1.9 %and_reduce_fusion = pred[32,384]{1,0:T(8,128)(4,1)S(1)} fusion(s32[32,384]{1,0:T(8,128)S(1)} %eq.116, s32[32,16]{1,0:T(8,128)S(1)} %get-tuple-element.106, s32[32,16]{1,0:T(8,128)S(1)} %get-tuple-element.107, s32[32,16]{1,0:T(8,128)S(1)} %get-tuple-element.108, s32[32,16]{1,0:T(8,128)S(1)} %get-tuple-element.109, s32[32,16]{1,0:T(8,128)S(1)} %get-tuple-element.110, ...), kind=kLoop, calls=%fused_computation.27 | loop fusion | flops 6279168 | bytes 126976 | tf_op jit(solution)/shard_map/reduce_or | solution.py:55
  16.0 0.8 select_reduce_fusion.2
  17.6 0.1 fusion.23
  17.7 0.1 fusion.21
  17.7 0.1 fusion.24
  17.9 0.1 fusion.25
  18.0 0.1 fusion.22
  18.3 0.2 concatenate.171
  18.6 0.2 fusion
  18.9 0.1 broadcast_compare_fusion
  19.0 131.9 %conditional.1 = (f32[1024,512]{1,0:T(8,128)S(1)}) conditional(s32[]{:T(128)} %convert_element_type.15, (pred[16,8,512]{2,1,0:T(8,128)(4,1)S(1)}, pred[16,8,512]{2,1,0:T(8,128)(4,1)S(1)}, s32[384]{0:T(512)S(1)}, s32[8,64]{1,0:T(8,128)S(1)}, bf16[1024,512]{1,0:T(8,128)(2,1)S(1)}, /*index=5*/bf16[1024,512]{1,0:T(8,128)(2,1)}, ...), branch_computations={%region_2.4_spmd.clone, %region_4.6_spmd.clone} | conditional | flops 1573632 | bytes 160776 | solution.py:260
  19.2 0.7 add_select_fusion.1
  19.9 2.2 %select_reduce_fusion.1 = s32[16,8,8]{2,1,0:T(8,128)S(1)} fusion(s32[512]{0:T(512)S(1)} %pad_add_fusion.1, pred[16,8,512]{2,1,0:T(8,128)(4,1)S(1)} %get-tuple-element.76, pred[16,8,512]{2,1,0:T(8,128)(4,1)S(1)} %get-tuple-element.75), kind=kLoop, calls=%fused_computation.12 | loop fusion | flops 1571840 | bytes 137216 | tf_op jit(solution)/shard_map/cond/branch_1_fun/reduce_sum | solution.py:92
  22.2 0.7 reshape.90.place_ref
  22.9 0.7 concatenate.175.send_ref
  23.5 127.4 %branch_1_fun.1 = f32[1024,512]{1,0:T(8,128)S(1)} custom-call(s32[1024]{0:T(1024)} %reshape.90.place_ref, s32[176]{0:T(256)} %concatenate.175.send_ref, bf16[1024,512]{1,0:T(8,128)(2,1)S(1)} %get-tuple-element.79.kernel_ref, bf16[1024,512]{1,0:T(8,128)(2,1)} %get-tuple-element.80.margin_ref, bf16[1024,512]{1,0:T(8,128)(2,1)} %get-tuple-element.81.ham_ref), custom_call_target="tpu_custom_call" | custom-call | tf_op jit(solution)/shard_map/cond/branch_1_fun/pallas_call | solution.py:231
  151.0 1.3 copy.56
  (42 shorter events, 0.6 us)
Async XLA Ops:
  12.7 3.4 %copy-start.1 = (bf16[384,384]{1,0:T(8,128)(2,1)S(1)}, bf16[384,384]{1,0:T(8,128)(2,1)}, u32[]{:S(2)}) copy-start(bf16[384,384]{1,0:T(8,128)(2,1)} %constant.60.clone) | copy-start | bytes 884740
  12.7 3.4 %copy-start.2 = (s32[384]{0:T(512)S(1)}, s32[384]{0:T(512)}, u32[]{:S(2)}) copy-start(s32[384]{0:T(512)} %constant.61.clone) | copy-start | bytes 4612
  13.0 5.6 %copy-start.3 = (bf16[8,384]{1,0:T(8,128)(2,1)S(1)}, bf16[8,384]{1,0:T(8,128)(2,1)}, u32[]{:S(2)}) copy-start(bf16[8,384]{1,0:T(8,128)(2,1)} %constant.62.clone) | copy-start | bytes 18436
  13.0 6.0 %copy-start = (bf16[1024,512]{1,0:T(8,128)(2,1)S(1)}, bf16[1024,512]{1,0:T(8,128)(2,1)}, u32[]{:S(2)}) copy-start(bf16[1024,512]{1,0:T(8,128)(2,1)} %param.11) | copy-start | bytes 3145732

commit v2 on v1

--- a/solution.py
+++ b/solution.py
@@ -22,11 +22,22 @@
 
 
 ROWS = [direction_rows(s, t) for s, t in DIRS]
-FULL = tuple(len(rows) * NB for rows in ROWS)
-SMALL = (32, 32, 24, 24, 16, 16, 16, 16)
-GHOST = sum(FULL)
-STARTS = np.cumsum((0,) + FULL)
-WIDEST = max(FULL)
+SIZES = [len(rows) * NB for rows in ROWS]
+GHOST = sum(SIZES)
+
+
+def messages(along_gy):
+    if along_gy == 2:
+        return ((0, 1), (2,), (3,), (4, 5), (6, 7))
+    return tuple((d,) for d in range(len(DIRS)))
+
+
+def full_caps(along_gy):
+    return tuple(sum(SIZES[d] for d in group) for group in messages(along_gy))
+
+
+def small_caps(along_gy):
+    return (48, 24, 24, 20, 20) if along_gy == 2 else (32, 32, 24, 24, 16, 16, 16, 16)
 
 
 def starts_of(caps):
@@ -35,47 +46,53 @@
 
 def tables(columns, along_gx, along_gy, gx_index, gy_index):
     count = along_gx * along_gy
-    ids = jnp.arange(count * BLK_DEV, dtype=jnp.int32).reshape(along_gx, along_gy, BLK_DEV)
-    slots = columns.reshape(along_gx, along_gy, BLK_DEV, NB)
-    ghost_ids, ghost_slots = [], []
-    for (s, t), rows in zip(DIRS, ROWS):
-        for source, kept in ((ids[..., None], ghost_ids), (slots, ghost_slots)):
-            moved = jnp.roll(source, (-s, -t), (0, 1))
-            pieces = [moved[:, :, r : r + EDGE] for r in rows[::EDGE]]
-            kept.append(jnp.concatenate(pieces, axis=2))
-    ghost_slots = jnp.concatenate(ghost_slots, axis=2).reshape(count, GHOST)
-    ghost_ids = jnp.concatenate(ghost_ids, axis=2)
-    ghost_ids = jnp.broadcast_to(ghost_ids, ghost_ids.shape[:3] + (NB,)).reshape(count, GHOST)
-    live = jnp.where(slots >= 0, slots, -2).reshape(count, BLK_DEV, NB)
+    groups, full = messages(along_gy), full_caps(along_gy)
+    bounds = starts_of(full)
+    widest = max(full)
+    ids = np.arange(count * BLK_DEV, dtype=np.int32).reshape(along_gx, along_gy, BLK_DEV)
+    ids = np.repeat(ids, NB, axis=2)
+    lanes = columns.reshape(along_gx, along_gy, OWN)
+
+    def ghosts(lib, source):
+        kept = []
+        for (s, t), rows in zip(DIRS, ROWS):
+            moved = lib.roll(source, (-s, -t), (0, 1))
+            kept += [moved[:, :, r * NB : (r + EDGE) * NB] for r in rows[::EDGE]]
+        return lib.concatenate(kept, axis=2).reshape(count, GHOST)
+
+    ghost_ids = jnp.asarray(ghosts(np, ids))
+    ghost_slots = ghosts(jnp, lanes)
+    slots = columns.reshape(count, BLK_DEV, NB)
+    live = jnp.where(slots >= 0, slots, -2)
     names_row = jnp.zeros((count, BLK_DEV, GHOST), bool)
     names_column = jnp.zeros((count, BLK_DEV, GHOST), bool)
     for b in range(NB):
         names_row |= live[:, :, b, None] == ghost_ids[:, None, :]
         names_column |= live[:, :, b, None] == ghost_slots[:, None, :]
     need = jnp.any(names_row & names_column, axis=1)
-    segment = np.repeat(np.arange(len(DIRS)), FULL)
+    segment = np.repeat(np.arange(len(groups)), full)
     before = (segment[:, None] == segment[None, :]) & (np.arange(GHOST)[:, None] < np.arange(GHOST)[None, :])
     ones = need.astype(jnp.bfloat16)
     rank = jnp.dot(ones, jnp.asarray(before, jnp.bfloat16), preferred_element_type=jnp.float32).astype(jnp.int32)
-    limit = jnp.asarray(np.repeat(SMALL, FULL).astype(np.int32))
+    limit = jnp.asarray(np.repeat(small_caps(along_gy), full).astype(np.int32))
     fits = jnp.all(jnp.where(need, rank < limit, True))
     ranked = jnp.where(need, rank, -1)
 
     own_rank = lax.dynamic_index_in_dim(ranked, gx_index * along_gy + gy_index, 0, keepdims=False)
     by_device = ranked.reshape(along_gx, along_gy, GHOST)
     sent_rank = jnp.concatenate(
-        [jnp.roll(by_device[:, :, lo:hi], (s, t), (0, 1)) for (s, t), lo, hi in zip(DIRS, STARTS[:-1], STARTS[1:])],
+        [jnp.roll(by_device[:, :, lo:hi], (s, t), (0, 1)) for (s, t), lo, hi in zip([DIRS[g[0]] for g in groups], bounds[:-1], bounds[1:])],
         axis=2,
     ).reshape(count, GHOST)
     sent_rank = lax.dynamic_index_in_dim(sent_rank, gx_index * along_gy + gy_index, 0, keepdims=False)
     block = np.concatenate([[1 + r * NB + c for r in rows for c in range(NB)] for rows in ROWS])
-    chosen = (sent_rank[:, None] == jnp.arange(WIDEST, dtype=jnp.int32)[None, :]).astype(jnp.bfloat16)
-    weights = (segment[None, :] == np.arange(len(DIRS))[:, None]) * block[None, :]
+    chosen = (sent_rank[:, None] == jnp.arange(widest, dtype=jnp.int32)[None, :]).astype(jnp.bfloat16)
+    weights = (segment[None, :] == np.arange(len(groups))[:, None]) * block[None, :]
     sends = jnp.dot(jnp.asarray(weights, jnp.bfloat16), chosen, preferred_element_type=jnp.float32)
     sends = sends.astype(jnp.int32)
 
     me = gx_index * along_gy + gy_index
-    own_slots = lax.dynamic_index_in_dim(columns.reshape(count, BLK_DEV, NB), me, 0, keepdims=False)
+    own_slots = lax.dynamic_index_in_dim(slots, me, 0, keepdims=False)
     my_ghost_slots = lax.dynamic_index_in_dim(ghost_slots, me, 0, keepdims=False)
     my_ghost_ids = lax.dynamic_index_in_dim(ghost_ids, me, 0, keepdims=False)
     flat_slots = jnp.concatenate([own_slots.reshape(-1), my_ghost_slots])
@@ -85,7 +102,7 @@
     of_column = wanted[:, :, None] == flat_slots[None, None, :]
 
     def places(caps):
-        offset = np.repeat(starts_of(caps)[:-1], FULL) + 1 + OWN
+        offset = np.repeat(starts_of(caps)[:-1], full) + 1 + OWN
         ghost = jnp.where(own_rank >= 0, own_rank + jnp.asarray(offset, jnp.int32), 0)
         place = jnp.concatenate([1 + jnp.arange(OWN, dtype=jnp.int32), ghost])
         both = of_row[:, :, None, :] & of_column[:, None, :, :]
@@ -103,8 +120,9 @@
     pair_starts = [v // 2 for v in starts_of(caps)]
     pairs = pair_starts[-1]
     gx_index, gy_index = lax.axis_index("gx"), lax.axis_index("gy")
+    served = [DIRS[group[0]] for group in messages(along_gy)]
     targets = [
-        (lax.rem(gx_index - s + along_gx, along_gx), lax.rem(gy_index - t + along_gy, along_gy)) for s, t in DIRS
+        (lax.rem(gx_index - s + along_gx, along_gx), lax.rem(gy_index - t + along_gy, along_gy)) for s, t in served
     ]
     low = lax.broadcasted_iota(jnp.int32, (BS, 2 * BS), 1) < BS
 
@@ -184,14 +202,14 @@
         out_ref[rows, cols] = result
 
     barrier = pltpu.get_barrier_semaphore()
-    for target, (s, t) in zip(targets, DIRS):
+    for target in targets:
         pl.semaphore_signal(barrier, inc=1, device_id=target, device_id_type=pl.DeviceIdType.MESH)
     zero = jnp.zeros((BS, 2 * BS), jnp.bfloat16)
     blocks[0] = zero
     other[0] = zero
     own(margin_ref, blocks)
     first = exchange(0, blocks)
-    pl.semaphore_wait(barrier, len(DIRS))
+    pl.semaphore_wait(barrier, len(targets))
     for copy in first:
         copy.start()
     own(kernel_ref, other)
@@ -240,8 +258,8 @@
             pltpu.VMEM((rows, width), jnp.bfloat16),
             pltpu.VMEM((2, pairs, BS, 2 * BS), jnp.bfloat16),
             pltpu.VMEM((4, pairs, BS, 2 * BS), jnp.bfloat16),
-            pltpu.SemaphoreType.DMA((4, len(DIRS))),
-            pltpu.SemaphoreType.DMA((4, len(DIRS))),
+            pltpu.SemaphoreType.DMA((4, len(caps))),
+            pltpu.SemaphoreType.DMA((4, len(caps))),
         ],
         compiler_params=pltpu.CompilerParams(
             collective_id=collective_id, has_side_effects=True, vmem_limit_bytes=56 * 2**20
@@ -257,7 +275,7 @@
             sizes, caps, collective_id, places(caps), send_list(caps), kernel, margin, hamiltonian
         )
 
-    return lax.cond(fits, run(SMALL, 0), run(FULL, 1))
+    return lax.cond(fits, run(small_caps(sizes[1]), 0), run(full_caps(sizes[1]), 1))
 
 
 def solution(mesh):

time: 153 us -> 114 us (0.75)
  Pallas kernels: 127 us -> 97.4 us
  local copies, waits for them, and re-layouts: 14.5 us -> 8.42 us
  other arithmetic: 8.1 us -> 5.5 us
    pallas_call x1, Pallas kernels: 127 us -> 97.4 us  [call(): pl.pallas_call(functools.partial(purify, sizes, caps), out_shape=jax.Shap...]
    concatenate x3, local copies, waits for them, and re-layouts: 5.58 us -> 0.28 us  [the longest x1 0.26 us: ghosts(): return lib.concatenate(kept, axis=2).reshape(count, GHOST)]
    concatenate x10 -> x2, other arithmetic: 2.82 us -> 0.34 us  [ghosts(): moved = lib.roll(source, (-s, -t), (0, 1))]
where the time goes in v2:
time: 114 us; the launch traced here: 113 us
  Pallas kernels  97.4 us (85%)
  local copies, waits for them, and re-layouts  8.42 us (7%)
  other arithmetic  5.5 us (5%)
    pallas_call x1, Pallas kernels, call(): pl.pallas_call(functools.partial(purify, sizes, caps), out_shape=jax.Shap...  97.4 us
    slice x13, local copies, waits for them, and re-layouts, ghosts(): moved = lib.roll(source, (-s, -t), (0, 1))  2.58 us

profile of v2, /device:TPU:1, one launch (start us, length us, event | category | flops | bytes accessed | tf_op | source)
XLA Modules:
  0.0 113.5 jit_solution(7973304322165556630)
XLA Ops:
  0.0 0.0 copy-start.3
  0.0 0.0 copy-start.4
  0.0 0.0 copy-start.1
  0.0 0.8 dynamic-slice_reduce_fusion.3
  0.8 0.1 broadcast_in_dim.66
  0.9 0.1 reshape.54
  1.0 0.8 fusion.12
  1.8 0.1 copy.32
  1.9 0.1 slice.267
  2.0 0.1 copy.29
  2.0 0.1 slice.260
  2.1 0.9 fusion.13
  3.0 0.8 reshape.52
  3.9 0.0 copy-start.5
  3.9 0.0 copy-start
  3.9 0.1 copy.33
  4.0 0.1 copy.34
  4.1 0.1 reshape.55
  4.2 0.1 copy.31
  4.3 0.2 slice.265
  4.5 0.1 copy.30
  4.6 0.2 slice.262
  4.8 0.1 slice.317
  4.9 0.2 pad_add_fusion.2
  5.1 0.0 copy-done.1
  5.1 0.1 copy.28
  5.2 0.2 reshape.53
  5.4 0.2 pad_add_fusion.4
  5.6 0.3 concatenate.91
  5.9 0.0 copy-done.3
  5.9 1.9 %and_reduce_fusion = pred[32,384]{1,0:T(8,128)(4,1)S(1)} fusion(s32[32,384]{1,0:T(8,128)S(1)} %eq.113, s32[32,16]{1,0:T(8,128)S(1)} %get-tuple-element.98, s32[32,16]{1,0:T(8,128)S(1)} %get-tuple-element.99, s32[32,16]{1,0:T(8,128)S(1)} %get-tuple-element.100, s32[32,16]{1,0:T(8,128)S(1)} %get-tuple-element.101, s32[32,16]{1,0:T(8,128)S(1)} %get-tuple-element.102, ...), kind=kLoop, calls=%fused_computation.21 | loop fusion | flops 6279168 | bytes 126976 | tf_op jit(solution)/shard_map/reduce_or | solution.py:72
  7.9 0.0 copy-done.4
  7.9 0.0 copy-done.2
  7.9 0.8 select_reduce_fusion.2
  9.4 0.1 fusion.7
  9.5 0.1 fusion.8
  9.8 0.1 concatenate.101
  10.0 0.0 copy-done.5
  10.0 0.2 fusion
  10.2 0.1 broadcast_compare_fusion
  10.4 0.0 copy-done
  10.4 101.7 %conditional.1 = (f32[1024,512]{1,0:T(8,128)S(1)}) conditional(s32[]{:T(128)} %convert_element_type.15, (pred[16,8,512]{2,1,0:T(8,128)(4,1)S(1)}, pred[16,8,512]{2,1,0:T(8,128)(4,1)S(1)}, s32[384]{0:T(512)S(1)}, s32[5,128]{1,0:T(8,128)S(1)}, bf16[1024,512]{1,0:T(8,128)(2,1)S(1)}, /*index=5*/bf16[1024,512]{1,0:T(8,128)(2,1)}, ...), branch_computations={%region_2.4_spmd.clone, %region_4.6_spmd.clone} | conditional | flops 1573632 | bytes 160776 | solution.py:278
  10.4 0.7 add_select_fusion.1
  11.1 2.2 %select_reduce_fusion.1 = s32[16,8,8]{2,1,0:T(8,128)S(1)} fusion(s32[512]{0:T(512)S(1)} %pad_add_fusion.1, pred[16,8,512]{2,1,0:T(8,128)(4,1)S(1)} %get-tuple-element.76, pred[16,8,512]{2,1,0:T(8,128)(4,1)S(1)} %get-tuple-element.75), kind=kLoop, calls=%fused_computation.9 | loop fusion | flops 1571840 | bytes 137216 | tf_op jit(solution)/shard_map/cond/branch_1_fun/reduce_sum | solution.py:109
  13.4 0.7 reshape.59.place_ref
  14.1 0.6 concatenate.105.send_ref
  14.7 97.4 %branch_1_fun.1 = f32[1024,512]{1,0:T(8,128)S(1)} custom-call(s32[1024]{0:T(1024)} %reshape.59.place_ref, s32[136]{0:T(256)} %concatenate.105.send_ref, bf16[1024,512]{1,0:T(8,128)(2,1)S(1)} %get-tuple-element.79.kernel_ref, bf16[1024,512]{1,0:T(8,128)(2,1)} %get-tuple-element.80.margin_ref, bf16[1024,512]{1,0:T(8,128)(2,1)} %get-tuple-element.81.ham_ref), custom_call_target="tpu_custom_call" | custom-call | tf_op jit(solution)/shard_map/cond/branch_1_fun/pallas_call | solution.py:249
  112.1 1.3 %copy.40 = f32[1024,512]{1,0:T(8,128)} copy(f32[1024,512]{1,0:T(8,128)S(1)} %get-tuple-element.56) | data formatting | bytes 4194304
  (35 shorter events, 0.5 us)
Async XLA Ops:
  0.0 5.9 %copy-start.3 = (s32[32,384]{1,0:T(8,128)S(1)}, s32[32,384]{1,0:T(8,128)}, u32[]{:S(2)}) copy-start(s32[32,384]{1,0:T(8,128)} %constant.62.clone) | copy-start | bytes 147460
  0.0 7.9 %copy-start.4 = (s32[384]{0:T(512)S(1)}, s32[384]{0:T(512)}, u32[]{:S(2)}) copy-start(s32[384]{0:T(512)} %constant.64.clone) | copy-start | bytes 4612
  0.0 7.9 %copy-start.2 = (bf16[384,384]{1,0:T(8,128)(2,1)S(1)}, bf16[384,384]{1,0:T(8,128)(2,1)}, u32[]{:S(2)}) copy-start(bf16[384,384]{1,0:T(8,128)(2,1)} %constant.63.clone) | copy-start | bytes 884740
  0.0 5.1 %copy-start.1 = (s32[512,8]{0,1:T(8,128)S(1)}, s32[512,8]{0,1:T(8,128)}, u32[]{:S(2)}) copy-start(s32[512,8]{0,1:T(8,128)} %param.15) | copy-start | bytes 49156
  3.9 6.1 %copy-start.5 = (bf16[5,384]{1,0:T(8,128)(2,1)S(1)}, bf16[5,384]{1,0:T(8,128)(2,1)}, u32[]{:S(2)}) copy-start(bf16[5,384]{1,0:T(8,128)(2,1)} %constant.65.clone) | copy-start | bytes 11524
  3.9 6.5 %copy-start = (bf16[1024,512]{1,0:T(8,128)(2,1)S(1)}, bf16[1024,512]{1,0:T(8,128)(2,1)}, u32[]{:S(2)}) copy-start(bf16[1024,512]{1,0:T(8,128)(2,1)} %param.12) | copy-start | bytes 3145732
